TPU v7x, 32 devices: a whole 2x2x4 slice. The times are simulated.
32 devices in a mesh: dp: 8 (over z, y), mp: 4 (over x, core).
Axes of the slice: x: 2, y: 2, z: 4, core: 2. Of those that a mesh axis runs over, the one named last changes fastest.
Arguments:
- block_input: bfloat16 [8, 2048, 768], P('dp', 'mp'), may hold values from -6 to 6
- out_cotangent: bfloat16 [8, 2048, 768], P('dp', 'mp'), may hold values from -6 to 6
- lengths: int32 [8], P('dp'), may hold values from 1024 to 2048, as said below
- w_qkv: float32 [768, 3, 768], P('dp', None, 'mp'), may hold values from -0.21875 to 0.21875
- w_out: float32 [768, 768], P('mp', 'dp'), may hold values from -1.75 to 1.75
- w_up: float32 [768, 3072], P('dp', 'mp'), may hold values from -0.21875 to 0.21875
- w_down: float32 [3072, 768], P('mp', 'dp'), may hold values from -0.109375 to 0.109375
- pair_bias: float32 [2048, 256], P(('dp', 'mp')), may hold values from -1.5 to 1.5
- norm_gains: float32 [2, 768], replicated, may hold values from 0.5 to 1.5
- first_qkv: float32 [768, 3, 768], P('dp', None, 'mp'), may hold values from -0.625 to 0.625
- first_out: float32 [768, 768], P('mp', 'dp'), may hold values from -0.125 to 0.125
- first_up: float32 [768, 3072], P('dp', 'mp'), may hold values from -0.625 to 0.625
- first_down: float32 [3072, 768], P('mp', 'dp'), may hold values from -0.625 to 0.625
- first_bias: float32 [2048, 256], P(('dp', 'mp')), may hold values from -0.03125 to 0.03125
- first_gains: float32 [2, 768], replicated, may hold values from -0.625 to 0.625
- second_qkv: float32 [768, 3, 768], P('dp', None, 'mp'), may hold values from 0.002 to 0.03
- second_out: float32 [768, 768], P('mp', 'dp'), may hold values from 0.0001 to 0.0015
- second_up: float32 [768, 3072], P('dp', 'mp'), may hold values from 0.002 to 0.03
- second_down: float32 [3072, 768], P('mp', 'dp'), may hold values from 0.002 to 0.03
- second_bias: float32 [2048, 256], P(('dp', 'mp')), may hold values from 5e-05 to 0.00075
- second_gains: float32 [2, 768], replicated, may hold values from 0.002 to 0.03
Outputs:
- block_output: bfloat16 [8, 2048, 768], P('dp', 'mp')
- grad_input: float32 [8, 2048, 768], P('dp', 'mp')
- grad_qkv: float32 [768, 3, 768], P('dp', None, 'mp')
- grad_out: float32 [768, 768], P('mp', 'dp')
- grad_up: float32 [768, 3072], P('dp', 'mp')
- grad_down: float32 [3072, 768], P('mp', 'dp')
- grad_bias: float32 [2048, 256], P(('dp', 'mp'))
- grad_gains: float32 [2, 768], replicated
- newfirst_qkv: float32 [768, 3, 768], P('dp', None, 'mp')
- newfirst_out: float32 [768, 768], P('mp', 'dp')
- newfirst_up: float32 [768, 3072], P('dp', 'mp')
- newfirst_down: float32 [3072, 768], P('mp', 'dp')
- newfirst_bias: float32 [2048, 256], P(('dp', 'mp'))
- newfirst_gains: float32 [2, 768], replicated
- newsecond_qkv: float32 [768, 3, 768], P('dp', None, 'mp')
- newsecond_out: float32 [768, 768], P('mp', 'dp')
- newsecond_up: float32 [768, 3072], P('dp', 'mp')
- newsecond_down: float32 [3072, 768], P('mp', 'dp')
- newsecond_bias: float32 [2048, 256], P(('dp', 'mp'))
- newsecond_gains: float32 [2, 768], replicated
- update_qkv: float32 [768, 3, 768], P('dp', None, 'mp')
- update_out: float32 [768, 768], P('mp', 'dp')
- update_up: float32 [768, 3072], P('dp', 'mp')
- update_down: float32 [3072, 768], P('mp', 'dp')
- update_bias: float32 [2048, 256], P(('dp', 'mp'))
- update_gains: float32 [2, 768], replicated
- rms_stats: float32 [3], replicated
Inputs may be any that keep to these rules, and one draw needn't show every extreme that they name: `lengths`: every length is at least half of 2048, and one of them is exactly 2048.
All inputs are finite; a program needn't handle non-finite values.
Results may differ from a plain program's by a relative error of at most 0.012.
Values may be sent and summed in bfloat16 or wider, within the bound.
A program may use at most 192 MiB of HBM per device.

v0:
```python
import jax
import jax.numpy as jnp
from jax import lax
from jax.sharding import PartitionSpec as P

LEN = 2048
ADAM_STEP = 10
EPS = 1e-06
BETA_ONE = 0.9
BETA_TWO = 0.99
LEARN_RATE = 0.03
WEIGHT_DECAY = 0.1
ADAM_EPS = 1e-08


def skew_band(bias_rows):
    height, width = bias_rows.shape
    padded = jnp.concatenate(
        [
            jnp.zeros((height, 1), bias_rows.dtype),
            bias_rows[:, ::-1],
            jnp.zeros((height, height), bias_rows.dtype),
        ],
        axis=1,
    )
    return padded.reshape(-1)[: height * (height + width)].reshape(height, height + width)


def unskew_band(band_grad, window):
    height, width = band_grad.shape
    flat = jnp.concatenate([band_grad.reshape(-1), jnp.zeros((height,), band_grad.dtype)])
    return flat.reshape(height, width + 1)[:, 1 : window + 1][:, ::-1]


def mix_forward(queries, key_rows, value_rows, bias_low):
    seq_len, channels = queries.shape
    window = bias_low.shape[1]
    block = min(512, seq_len)
    exp_keys = jnp.exp(key_rows)
    front = jnp.zeros((window, channels), jnp.bfloat16)
    keys_pad = jnp.concatenate([front, exp_keys.astype(jnp.bfloat16)], axis=0)
    product_pad = jnp.concatenate([front, (exp_keys * value_rows).astype(jnp.bfloat16)], axis=0)

    def one_block(block_index):
        offset = block_index * block
        band_rows = skew_band(lax.dynamic_slice_in_dim(bias_low, offset, block, 0))
        key_block = lax.dynamic_slice_in_dim(keys_pad, offset, block + window, 0)
        product_block = lax.dynamic_slice_in_dim(product_pad, offset, block + window, 0)
        numerator = jnp.dot(band_rows, product_block, preferred_element_type=jnp.float32)
        denominator = jnp.dot(band_rows, key_block, preferred_element_type=jnp.float32)
        return (numerator, denominator)

    numerator, denominator = lax.map(one_block, jnp.arange(seq_len // block, dtype=jnp.int32))
    return (
        numerator.reshape(seq_len, channels),
        denominator.reshape(seq_len, channels),
        keys_pad,
        product_pad,
    )


def mix_backward(
    queries,
    key_rows,
    value_rows,
    numerator,
    denominator,
    keys_pad,
    product_pad,
    bias_low,
    grad_mixed,
):
    seq_len, channels = queries.shape
    window = bias_low.shape[1]
    block = min(512, seq_len)
    gate_sig = jax.nn.sigmoid(queries)
    mixed_ratio = numerator / denominator
    grad_query = grad_mixed * mixed_ratio * gate_sig * (1.0 - gate_sig)
    grad_numerator = (grad_mixed * gate_sig / denominator).astype(jnp.bfloat16)
    grad_denominator = (-grad_mixed * gate_sig * mixed_ratio / denominator).astype(jnp.bfloat16)

    def one_block(carry, block_index):
        product_sum, key_sum = carry
        offset = block_index * block
        band_rows = skew_band(lax.dynamic_slice_in_dim(bias_low, offset, block, 0))
        key_block = lax.dynamic_slice_in_dim(keys_pad, offset, block + window, 0)
        product_block = lax.dynamic_slice_in_dim(product_pad, offset, block + window, 0)
        upper_block = lax.dynamic_slice_in_dim(grad_numerator, offset, block, 0)
        lower_block = lax.dynamic_slice_in_dim(grad_denominator, offset, block, 0)
        product_part = jnp.einsum(
            "ij,ic->jc", band_rows, upper_block, preferred_element_type=jnp.float32
        )
        key_part = jnp.einsum(
            "ij,ic->jc", band_rows, lower_block, preferred_element_type=jnp.float32
        )
        product_sum = lax.dynamic_update_slice_in_dim(
            product_sum,
            lax.dynamic_slice_in_dim(product_sum, offset, block + window, 0) + product_part,
            offset,
            0,
        )
        key_sum = lax.dynamic_update_slice_in_dim(
            key_sum,
            lax.dynamic_slice_in_dim(key_sum, offset, block + window, 0) + key_part,
            offset,
            0,
        )
        band_grad = jnp.einsum(
            "ic,jc->ij", upper_block, product_block, preferred_element_type=jnp.float32
        )
        band_grad = band_grad + jnp.einsum(
            "ic,jc->ij", lower_block, key_block, preferred_element_type=jnp.float32
        )
        return ((product_sum, key_sum), unskew_band(band_grad, window))

    zeros_pad = jnp.zeros((seq_len + window, channels), jnp.float32)
    sums_pad, bias_blocks = lax.scan(
        one_block, (zeros_pad, zeros_pad), jnp.arange(seq_len // block, dtype=jnp.int32)
    )
    exp_keys = jnp.exp(key_rows)
    grad_product = sums_pad[0][window:]
    grad_keyexp = sums_pad[1][window:] + grad_product * value_rows
    grad_value = grad_product * exp_keys
    grad_key = grad_keyexp * exp_keys
    return (grad_query, grad_key, grad_value, bias_blocks.reshape(seq_len, window))


def rms_rescale(inputs):
    return lax.rsqrt(jnp.mean(inputs * inputs, axis=-1, keepdims=True) + EPS)


def norm_back(inputs, rescale, gain, grad_normed):
    scaled = grad_normed * gain
    grad_inputs = rescale * scaled - inputs * rescale * rescale * rescale * jnp.mean(
        scaled * inputs, axis=-1, keepdims=True
    )
    grad_gain = jnp.sum(grad_normed * inputs * rescale, axis=(0, 1))
    return (grad_inputs, grad_gain)


def gelu_tanh(pre_act):
    return jax.nn.gelu(pre_act, approximate=True)


def adam_step(param, grad, first, second, step_value, decay):
    new_first = BETA_ONE * first + (1.0 - BETA_ONE) * grad
    new_second = BETA_TWO * second + (1.0 - BETA_TWO) * grad * grad
    first_hat = new_first / (1.0 - jnp.power(jnp.float32(BETA_ONE), step_value))
    second_hat = new_second / (1.0 - jnp.power(jnp.float32(BETA_TWO), step_value))
    update = -LEARN_RATE * (first_hat / (jnp.sqrt(second_hat) + ADAM_EPS) + decay * param)
    return (new_first, new_second, update)


def shards(
    block_input,
    out_cotangent,
    lengths,
    w_qkv,
    w_out,
    w_up,
    w_down,
    pair_bias,
    norm_gains,
    first_qkv,
    first_out,
    first_up,
    first_down,
    first_bias,
    first_gains,
    second_qkv,
    second_out,
    second_up,
    second_down,
    second_bias,
    second_gains,
):
    query_weights, mixer_weights, hidden_weights, back_weights = (
        lax.all_gather(w_qkv.astype(jnp.bfloat16), "dp", axis=0, tiled=True),
        lax.all_gather(w_out.astype(jnp.bfloat16), "dp", axis=1, tiled=True),
        lax.all_gather(w_up.astype(jnp.bfloat16), "dp", axis=0, tiled=True),
        lax.all_gather(w_down.astype(jnp.bfloat16), "dp", axis=1, tiled=True),
    )
    bias_full = lax.all_gather(pair_bias, ("dp", "mp"), axis=0, tiled=True)
    exp_bias = jnp.exp(bias_full)
    bias_low = exp_bias.astype(jnp.bfloat16)
    seqs, quarter, width = block_input.shape
    dp_count = lax.axis_size("dp")
    positions = lax.axis_index("mp") * quarter + jnp.arange(quarter, dtype=jnp.int32)
    valid_mask = (positions[None, :] < lengths[:, None]).astype(jnp.float32)
    input_float = block_input.astype(jnp.float32)
    rescale_one = rms_rescale(input_float)
    normed_one = (input_float * rescale_one * norm_gains[0]).astype(jnp.bfloat16)
    full_one = lax.all_gather(normed_one, "mp", axis=1, tiled=True)
    projected = jnp.einsum(
        "std,dkc->stkc", full_one, query_weights, preferred_element_type=jnp.float32
    )
    queries = projected[:, :, 0]
    key_rows = projected[:, :, 1]
    value_rows = projected[:, :, 2]
    numerator, denominator, keys_pad, product_pad = jax.vmap(mix_forward, in_axes=(0, 0, 0, None))(
        queries, key_rows, value_rows, bias_low
    )
    mixed_low = (jax.nn.sigmoid(queries) * numerator / denominator).astype(jnp.bfloat16)
    attn_terms = jnp.einsum(
        "stc,cd->std", mixed_low, mixer_weights, preferred_element_type=jnp.float32
    )
    attn_rows = lax.psum_scatter(attn_terms, "mp", scatter_dimension=1, tiled=True)
    resid = input_float + attn_rows
    rescale_two = rms_rescale(resid)
    normed_two = (resid * rescale_two * norm_gains[1]).astype(jnp.bfloat16)
    full_two = lax.all_gather(normed_two, "mp", axis=1, tiled=True)
    pre_act = jnp.einsum(
        "std,df->stf", full_two, hidden_weights, preferred_element_type=jnp.float32
    )
    act_low = gelu_tanh(pre_act).astype(jnp.bfloat16)
    ffn_terms = jnp.einsum("stf,fd->std", act_low, back_weights, preferred_element_type=jnp.float32)
    ffn_rows = lax.psum_scatter(
        ffn_terms.astype(jnp.bfloat16), "mp", scatter_dimension=1, tiled=True
    ).astype(jnp.float32)
    block_output = (resid + ffn_rows).astype(jnp.bfloat16)
    cotangent = out_cotangent.astype(jnp.float32) * valid_mask[:, :, None]
    cot_low = cotangent.astype(jnp.bfloat16)
    grad_full = lax.all_gather(cot_low, "mp", axis=1, tiled=True)
    grad_act = jnp.einsum(
        "std,fd->stf", grad_full, back_weights, preferred_element_type=jnp.float32
    )
    grad_pre = jax.vjp(gelu_tanh, pre_act)[1](grad_act)[0].astype(jnp.bfloat16)
    normed_terms = jnp.einsum(
        "stf,df->std", grad_pre, hidden_weights, preferred_element_type=jnp.float32
    )
    grad_normed_two = lax.psum_scatter(normed_terms, "mp", scatter_dimension=1, tiled=True)
    grad_up_local = jnp.einsum(
        "std,stf->df", full_two, grad_pre, preferred_element_type=jnp.float32
    )
    grad_down_local = jnp.einsum(
        "stf,std->fd", act_low, grad_full, preferred_element_type=jnp.float32
    )
    grad_resid_norm, gain_two_grad = norm_back(resid, rescale_two, norm_gains[1], grad_normed_two)
    grad_resid = cotangent + grad_resid_norm
    resid_full = lax.all_gather(grad_resid.astype(jnp.bfloat16), "mp", axis=1, tiled=True)
    grad_mixed = jnp.einsum(
        "std,cd->stc", resid_full, mixer_weights, preferred_element_type=jnp.float32
    )
    grad_mixer = jnp.einsum(
        "stc,std->cd", mixed_low, resid_full, preferred_element_type=jnp.float32
    )
    grad_query, grad_key, grad_value, bias_parts = jax.vmap(
        mix_backward, in_axes=(0, 0, 0, 0, 0, 0, 0, None, 0)
    )(
        queries,
        key_rows,
        value_rows,
        numerator,
        denominator,
        keys_pad,
        product_pad,
        bias_low,
        grad_mixed,
    )
    grad_bias_local = jnp.sum(bias_parts, axis=0) * exp_bias
    grad_proj = jnp.stack([grad_query, grad_key, grad_value], axis=2).astype(jnp.bfloat16)
    input_terms = jnp.einsum(
        "stkc,dkc->std", grad_proj, query_weights, preferred_element_type=jnp.float32
    )
    grad_normed_one = lax.psum_scatter(
        input_terms.astype(jnp.bfloat16), "mp", scatter_dimension=1, tiled=True
    ).astype(jnp.float32)
    grad_projection = jnp.einsum(
        "std,stkc->dkc", full_one, grad_proj, preferred_element_type=jnp.float32
    )
    grad_input_norm, gain_one_grad = norm_back(
        input_float, rescale_one, norm_gains[0], grad_normed_one
    )
    grad_input = grad_resid + grad_input_norm
    owned_qkv, owned_out, owned_up, owned_down = (
        lax.psum_scatter(grad_projection, "dp", scatter_dimension=0, tiled=True),
        lax.psum_scatter(grad_mixer, "dp", scatter_dimension=1, tiled=True),
        lax.psum_scatter(grad_up_local, "dp", scatter_dimension=0, tiled=True),
        lax.psum_scatter(grad_down_local, "dp", scatter_dimension=1, tiled=True),
    )
    owned_bias = lax.psum_scatter(grad_bias_local, ("dp", "mp"), scatter_dimension=0, tiled=True)
    mask_cols = valid_mask[:, :, None]
    local_sums = jnp.stack(
        [
            jnp.sum(mask_cols * input_float * input_float),
            jnp.sum(mask_cols * attn_rows * attn_rows),
            jnp.sum(mask_cols * ffn_rows * ffn_rows),
            jnp.sum(valid_mask),
        ]
    )
    gain_grads, global_sums = lax.psum(
        (jnp.stack([gain_one_grad, gain_two_grad]), local_sums), ("dp", "mp")
    )
    grad_scale = float(seqs * dp_count * LEN) ** (-0.5)
    scaled = [
        owned_qkv * grad_scale,
        owned_out * grad_scale,
        owned_up * grad_scale,
        owned_down * grad_scale,
        owned_bias * grad_scale,
        gain_grads * grad_scale,
    ]
    params = (w_qkv, w_out, w_up, w_down, pair_bias, norm_gains)
    firsts = (first_qkv, first_out, first_up, first_down, first_bias, first_gains)
    seconds = (second_qkv, second_out, second_up, second_down, second_bias, second_gains)
    decays = (WEIGHT_DECAY, WEIGHT_DECAY, WEIGHT_DECAY, WEIGHT_DECAY, 0.0, 0.0)
    step_value = jnp.float32(ADAM_STEP)
    states = [
        adam_step(
            params[place], scaled[place], firsts[place], seconds[place], step_value, decays[place]
        )
        for place in range(6)
    ]
    rms_stats = jnp.sqrt(global_sums[:3] / (global_sums[3] * width))
    return (
        block_output,
        grad_input,
        scaled[0],
        scaled[1],
        scaled[2],
        scaled[3],
        scaled[4],
        scaled[5],
        states[0][0],
        states[1][0],
        states[2][0],
        states[3][0],
        states[4][0],
        states[5][0],
        states[0][1],
        states[1][1],
        states[2][1],
        states[3][1],
        states[4][1],
        states[5][1],
        states[0][2],
        states[1][2],
        states[2][2],
        states[3][2],
        states[4][2],
        states[5][2],
        rms_stats,
    )


def solution(mesh):
    placed = (
        P("dp", "mp", None),
        P("dp", "mp", None),
        P("dp"),
        P("dp", None, "mp"),
        P("mp", "dp"),
        P("dp", "mp"),
        P("mp", "dp"),
        P(("dp", "mp"), None),
        P(),
        P("dp", None, "mp"),
        P("mp", "dp"),
        P("dp", "mp"),
        P("mp", "dp"),
        P(("dp", "mp"), None),
        P(),
        P("dp", None, "mp"),
        P("mp", "dp"),
        P("dp", "mp"),
        P("mp", "dp"),
        P(("dp", "mp"), None),
        P(),
    )
    return jax.shard_map(
        shards,
        mesh=mesh,
        in_specs=placed,
        out_specs=(
            P("dp", "mp", None),
            P("dp", "mp", None),
            P("dp", None, "mp"),
            P("mp", "dp"),
            P("dp", "mp"),
            P("mp", "dp"),
            P(("dp", "mp"), None),
            P(),
            P("dp", None, "mp"),
            P("mp", "dp"),
            P("dp", "mp"),
            P("mp", "dp"),
            P(("dp", "mp"), None),
            P(),
            P("dp", None, "mp"),
            P("mp", "dp"),
            P("dp", "mp"),
            P("mp", "dp"),
            P(("dp", "mp"), None),
            P(),
            P("dp", None, "mp"),
            P("mp", "dp"),
            P("dp", "mp"),
            P("mp", "dp"),
            P(("dp", "mp"), None),
            P(),
            P(),
        ),
        check_vma=False,
    )
```

profile of v0, /device:TPU:0, one launch (start us, length us, event | category | flops | bytes accessed | tf_op | source)
XLA Modules:
  0.0 1117.6 jit_solution(440134953824008164)
XLA Ops:
  13.6 40.4 %all_gather.28 = bf16[768,3,192]{2,1,0:T(4,128)(2,1)S(1)} all-gather(bf16[96,3,192]{2,1,0:T(4,128)(2,1)S(1)} %copy.88), channel_id=1, replica_groups=mesh['dp'=8,'mp'=4] {'dp'}, dimensions={0}, use_global_device_ids=true | all-gather | bytes 995328 | tf_op jit(solution)/shard_map/all_gather | solution.py:178
  55.0 31.3 %all_gather.30 = bf16[192,768]{0,1:T(8,128)(2,1)S(1)} all-gather(bf16[192,96]{0,1:T(8,128)(2,1)S(1)} %copy.94), channel_id=1, replica_groups=mesh['dp'=8,'mp'=4] {'dp'}, dimensions={1}, use_global_device_ids=true | all-gather | bytes 331776 | tf_op jit(solution)/shard_map/all_gather | solution.py:179
  86.3 2.8 exponential_convert_fusion
  89.2 16.2 %all-gather.8.cloned.1.call-done = bf16[1,2048,768]{2,1,0:T(8,128)(2,1)} async-done(((bf16[1,512,768]{2,1,0:T(8,128)(2,1)}), bf16[1,2048,768]{2,1,0:T(8,128)(2,1)}) %all-gather.8.cloned.1.call-update) | async-done | bytes 3145744 | tf_op jit(solution)/shard_map/all_gather | solution.py:193
  105.3 3.9 fusion.52
  115.6 40.1 %while.36 = (s32[]{:T(128)}, f32[4,1,512,192]{2,3,1,0:T(8,128)}, f32[4,1,512,192]{2,3,1,0:T(8,128)}, s32[4]{0:T(128)S(1)}, bf16[2048,256]{1,0:T(8,128)(2,1)}, /*...) while((s32[]{:T(128)}, f32[4,1,512,192]{2,3,1,0:T(8,128)}, ...), condition=%wide.region_2.3_spmd, body=%wide.region_1.2_spmd.sunk | while | flops 304352256 | bytes 9974028 | solution.py:53
  162.3 5.7 convolution_bitcast_fusion.2
  170.2 56.4 %reduce-scatter.12.cloned.1.call-done = f32[1,512,768]{2,1,0:T(8,128)} async-done(((f32[1,2048,768]{2,1,0:T(8,128)}), f32[1,512,768]{2,1,0:T(8,128)}) %reduce-scatter.12.cloned.1.call-update) | async-done | bytes 1572880 | tf_op jit(solution)/shard_map/reduce_scatter | solution.py:207
  231.4 26.5 %all-gather.12.cloned.1.call-done = bf16[1,2048,768]{2,1,0:T(8,128)(2,1)} async-done(((bf16[1,512,768]{2,1,0:T(8,128)(2,1)}), bf16[1,2048,768]{2,1,0:T(8,128)(2,1)}) %all-gather.12.cloned.1.call-update) | async-done | bytes 3145744 | tf_op jit(solution)/shard_map/all_gather | solution.py:211
  257.9 7.5 fusion.50
  265.4 22.4 %all-gather.18.cloned.1.call-done = bf16[1,2048,768]{2,1,0:T(8,128)(2,1)} async-done(((bf16[1,512,768]{2,1,0:T(8,128)(2,1)}), bf16[1,2048,768]{2,1,0:T(8,128)(2,1)}) %all-gather.18.cloned.1.call-update) | async-done | bytes 3145744 | tf_op jit(solution)/shard_map/all_gather | solution.py:223
  287.8 8.2 fusion.44
  296.1 69.1 %reduce-scatter.24.cloned.1.call-done = f32[768,96]{0,1:T(8,128)} async-done(((f32[768,768]{0,1:T(8,128)}), f32[768,96]{0,1:T(8,128)}) %reduce-scatter.24.cloned.1.call-update) | async-done | bytes 294928 | tf_op jit(solution)/shard_map/reduce_scatter | solution.py:279
  367.5 41.4 %all-gather.16.cloned.1.call-done = bf16[768,768]{0,1:T(8,128)(2,1)} async-done(((bf16[768,96]{0,1:T(8,128)(2,1)}), bf16[768,768]{0,1:T(8,128)(2,1)}) %all-gather.16.cloned.1.call-update) | async-done | bytes 1179664 | tf_op jit(solution)/shard_map/all_gather | solution.py:181
  408.9 8.2 fusion.37
  418.9 4.6 convolution_bitcast_fusion.3
  424.7 8.5 fusion.54
  433.3 47.0 %reduce-scatter.16.cloned.1.call-done = f32[1,512,768]{2,1,0:T(8,128)} async-done(((f32[1,2048,768]{2,1,0:T(8,128)}), f32[1,512,768]{2,1,0:T(8,128)}) %reduce-scatter.16.cloned.1.call-update) | async-done | bytes 1572880 | tf_op jit(solution)/shard_map/reduce_scatter | solution.py:231
  482.7 37.9 %reduce-scatter.14.cloned.1.call-done = bf16[1,512,768]{2,1,0:T(8,128)(2,1)} async-done(((bf16[1,2048,768]{2,1,0:T(8,128)(2,1)}), bf16[1,512,768]{2,1,0:T(8,128)(2,1)}) %reduce-scatter.14.cloned.1.call-update) | async-done | bytes 786448 | tf_op jit(solution)/shard_map/reduce_scatter | solution.py:217
  520.6 5.3 fusion.105
  526.0 3.3 div.149
  534.0 4.2 fusion.48
  538.3 16.3 %all-gather.20.cloned.1.call-done = bf16[1,2048,768]{2,1,0:T(8,128)(2,1)} async-done(((bf16[1,512,768]{2,1,0:T(8,128)(2,1)}), bf16[1,2048,768]{2,1,0:T(8,128)(2,1)}) %all-gather.20.cloned.1.call-update) | async-done | bytes 3145744 | tf_op jit(solution)/shard_map/all_gather | solution.py:240
  554.6 5.9 fusion.96
  565.5 186.5 %while.37 = (s32[]{:T(128)}, f32[1,2304,192]{1,2,0:T(8,128)}, f32[1,2304,192]{1,2,0:T(8,128)}, f32[4,1,512,256]{3,2,1,0:T(8,128)}, s32[4]{0:T(128)S(1)}, /*index...) while((s32[]{:T(128)}, f32[1,2304,192]{1,2,0:T(8,128)}, ...), condition=%wide.region_10.11_spmd, body=%wide.region_8.10_spmd.sunk | while | flops 607325184 | bytes 47336400 | solution.py:117
  572.2 16.3 %pad_reduce_fusion.2 = f32[393728]{0:T(1024)S(1)} fusion(f32[1,393216]{1,0:T(1,128)S(1)} %bitcast.305), kind=kLoop, calls=%fused_computation.13.clone.1 | loop fusion | bytes 3147776 | tf_op jit(solution)/shard_map/vmap()/while/body/eval_jaxpr/concatenate | solution.py:31
  596.9 2.7 fusion.157
  599.7 4.4 scatter.13
  606.2 5.9 scatter.12
  619.6 16.3 %pad_reduce_fusion.2 = f32[393728]{0:T(1024)S(1)} fusion(f32[1,393216]{1,0:T(1,128)S(1)} %bitcast.305), kind=kLoop, calls=%fused_computation.13.clone.1 | loop fusion | bytes 3147776 | tf_op jit(solution)/shard_map/vmap()/while/body/eval_jaxpr/concatenate | solution.py:31
  647.0 4.4 scatter.13
  653.5 5.9 scatter.12
  667.0 16.3 %pad_reduce_fusion.2 = f32[393728]{0:T(1024)S(1)} fusion(f32[1,393216]{1,0:T(1,128)S(1)} %bitcast.305), kind=kLoop, calls=%fused_computation.13.clone.1 | loop fusion | bytes 3147776 | tf_op jit(solution)/shard_map/vmap()/while/body/eval_jaxpr/concatenate | solution.py:31
  694.4 4.3 scatter.13
  700.8 5.3 scatter.12
  713.6 16.3 %pad_reduce_fusion.2 = f32[393728]{0:T(1024)S(1)} fusion(f32[1,393216]{1,0:T(1,128)S(1)} %bitcast.305), kind=kLoop, calls=%fused_computation.13.clone.1 | loop fusion | bytes 3147776 | tf_op jit(solution)/shard_map/vmap()/while/body/eval_jaxpr/concatenate | solution.py:31
  740.9 3.7 scatter.13
  746.7 3.9 scatter.12
  752.1 3.7 fusion.94
  756.8 4.1 fusion.38
  762.5 3.3 bitcast_multiply_fusion
  767.1 5.4 fusion.55
  775.8 38.9 %reduce-scatter.28.cloned.1.call-done = f32[96,192]{1,0:T(8,128)} async-done(((f32[768,192]{1,0:T(8,128)}), f32[96,192]{1,0:T(8,128)}) %reduce-scatter.28.cloned.1.call-update) | async-done | bytes 73744
  816.5 69.8 %reduce-scatter.20.cloned.1.call-done = f32[96,3,192]{2,0,1:T(8,128)} async-done(((f32[768,3,192]{2,0,1:T(8,128)}), f32[96,3,192]{2,0,1:T(8,128)}) %reduce-scatter.20.cloned.1.call-update) | async-done | bytes 221200 | tf_op jit(solution)/shard_map/reduce_scatter | solution.py:276
  888.5 135.4 %reduce-scatter.26.cloned.1.call-done = f32[64,256]{1,0:T(8,128)} async-done(((f32[2048,256]{1,0:T(8,128)}), f32[64,256]{1,0:T(8,128)}) %reduce-scatter.26.cloned.1.call-update) | async-done | bytes 65552 | tf_op jit(solution)/shard_map/reduce_scatter | solution.py:281
  1025.4 34.9 %reduce-scatter.18.cloned.1.call-done = bf16[1,512,768]{2,1,0:T(8,128)(2,1)} async-done(((bf16[1,2048,768]{2,1,0:T(8,128)(2,1)}), bf16[1,512,768]{2,1,0:T(8,128)(2,1)}) %reduce-scatter.18.cloned.1.call-update) | async-done | bytes 786448 | tf_op jit(solution)/shard_map/reduce_scatter | solution.py:265
  1065.7 39.4 %all-reduce.3 = (f32[2,768]{1,0:T(2,128)S(1)}, f32[4]{0:T(128)S(1)}) all-reduce(f32[2,768]{1,0:T(2,128)S(1)} %pad_maximum_fusion.3, f32[4]{0:T(128)S(1)} %pad_maximum_fusion.4), channel_id=1, replica_groups=mesh['dp'=8,'mp'=4] {'dp','mp'}, use_global_device_ids=true, to_apply=%region_20.21 | all-reduce | flops 1540 | bytes 12320 | tf_op jit(solution)/shard_map/psum | solution.py:291
  1107.4 2.8 fusion.65
  (351 shorter events, 177.3 us)
Async XLA Ops:
  8.0 78.3 %all-gather.10.cloned.1.call-start = ((), (), s32[]{:S(2)}) async-start(), calls=%async_computation.10 | async-start | bytes 2162688 | tf_op jit(solution)/shard_map/all_gather | solution.py:183
  8.8 96.6 %all-gather.8.cloned.1.call-start = ((), (), s32[]{:S(2)}) async-start(), calls=%async_computation.9 | async-start | bytes 3932160 | tf_op jit(solution)/shard_map/all_gather | solution.py:193
  13.4 213.3 %reduce-scatter.12.cloned.1.call-start = ((), (), s32[]{:S(2)}) async-start(), calls=%async_computation.11 | async-start | bytes 7864320 | tf_op jit(solution)/shard_map/reduce_scatter | solution.py:207
  54.9 50.5 %copy-start.20 = (bf16[768,3,192]{0,2,1:T(8,128)(2,1)}, bf16[768,3,192]{0,2,1:T(8,128)(2,1)S(1)}, u32[]{:S(2)}) copy-start(bf16[768,3,192]{0,2,1:T(8,128)(2,1)S(1)} %copy.89) | copy-start | bytes 2654212
  168.0 58.6 %copy-start.2 = (bf16[1,512,768]{2,1,0:T(8,128)(2,1)S(1)}, bf16[1,512,768]{2,1,0:T(8,128)(2,1)}, u32[]{:S(2)}) copy-start(bf16[1,512,768]{2,1,0:T(8,128)(2,1)} %param.29) | copy-start | bytes 2359300
  168.0 63.3 %all-gather.14.cloned.1.call-start = ((), (), s32[]{:S(2)}) async-start(), calls=%async_computation.13 | async-start | bytes 1327104 | tf_op jit(solution)/shard_map/all_gather | solution.py:180
  169.7 88.2 %all-gather.12.cloned.1.call-start = ((), (), s32[]{:S(2)}) async-start(), calls=%async_computation.12 | async-start | bytes 3932160 | tf_op jit(solution)/shard_map/all_gather | solution.py:211
  229.4 58.4 %all-gather.18.cloned.1.call-start = ((), (), s32[]{:S(2)}) async-start(), calls=%async_computation.16 | async-start | bytes 3932160 | tf_op jit(solution)/shard_map/all_gather | solution.py:223
  231.3 133.9 %reduce-scatter.24.cloned.1.call-start = ((), (), s32[]{:S(2)}) async-start(), calls=%async_computation.22 | async-start | bytes 2654208 | tf_op jit(solution)/shard_map/reduce_scatter | solution.py:279
  296.1 69.1 %copy-start.27 = (f32[768,96]{0,1:T(8,128)S(1)}, f32[768,96]{0,1:T(8,128)}, u32[]{:S(2)}) copy-start(f32[768,96]{0,1:T(8,128)} %param.35) | copy-start | bytes 884740
  296.1 69.1 %copy-start.28 = (f32[768,96]{0,1:T(8,128)S(1)}, f32[768,96]{0,1:T(8,128)}, u32[]{:S(2)}) copy-start(f32[768,96]{0,1:T(8,128)} %param.47) | copy-start | bytes 884740
  296.1 69.1 %copy-start.29 = (f32[768,96]{0,1:T(8,128)S(1)}, f32[768,96]{0,1:T(8,128)}, u32[]{:S(2)}) copy-start(f32[768,96]{0,1:T(8,128)} %param.41) | copy-start | bytes 884740
  296.1 112.8 %all-gather.16.cloned.1.call-start = ((), (), s32[]{:S(2)}) async-start(), calls=%async_computation.14 | async-start | bytes 1327104 | tf_op jit(solution)/shard_map/all_gather | solution.py:181
  367.4 51.5 %copy-start.51 = (bf16[768,768]{1,0:T(8,128)(2,1)S(1)}, bf16[768,768]{1,0:T(8,128)(2,1)}, u32[]{:S(2)}) copy-start(bf16[768,768]{1,0:T(8,128)(2,1)} %all-gather.14.cloned.1.call-done) | copy-start | bytes 3538948
  367.4 112.9 %reduce-scatter.16.cloned.1.call-start = ((), (), s32[]{:S(2)}) async-start(), calls=%async_computation.17 | async-start | bytes 7864320 | tf_op jit(solution)/shard_map/reduce_scatter | solution.py:231
  423.5 97.1 %reduce-scatter.14.cloned.1.call-start = ((), (), s32[]{:S(2)}) async-start(), calls=%async_computation.15 | async-start | bytes 3932160 | tf_op jit(solution)/shard_map/reduce_scatter | solution.py:217
  433.3 87.3 %copy-start.6 = (f32[1,512,768]{2,1,0:T(8,128)S(1)}, f32[1,512,768]{2,1,0:T(8,128)}, u32[]{:S(2)}) copy-start(f32[1,512,768]{2,1,0:T(8,128)} %reduce-scatter.12.cloned.1.call-done) | copy-start | bytes 4718596
  433.3 121.3 %all-gather.20.cloned.1.call-start = ((), (), s32[]{:S(2)}) async-start(), calls=%async_computation.18 | async-start | bytes 3932160 | tf_op jit(solution)/shard_map/all_gather | solution.py:240
  525.9 247.3 %reduce-scatter.22.cloned.1.call-start = ((), (), s32[]{:S(2)}) async-start(), calls=%async_computation.21 | async-start | bytes 2654208 | tf_op jit(solution)/shard_map/reduce_scatter | solution.py:278
  534.0 20.6 %copy-start.15 = (f32[24,8,4,512]{3,1,2,0:T(8,128)S(1)}, f32[24,8,4,512]{3,1,2,0:T(8,128)}, u32[]{:S(2)}) copy-start(f32[24,8,4,512]{3,1,2,0:T(8,128)} %copy-done.14) | copy-start | bytes 4718596
  538.2 16.4 %copy-start.13 = (f32[24,8,4,512]{3,1,2,0:T(8,128)S(1)}, f32[24,8,4,512]{3,1,2,0:T(8,128)}, u32[]{:S(2)}) copy-start(f32[24,8,4,512]{3,1,2,0:T(8,128)} %copy-done.12) | copy-start | bytes 4718596
  538.2 276.5 %reduce-scatter.28.cloned.1.call-start = ((), (), s32[]{:S(2)}) async-start(), calls=%async_computation.24 | async-start | bytes 884736
  554.6 5.9 copy-start.22
  554.6 5.9 copy-start.50
  596.9 7.2 copy-start
  644.3 7.1 copy-start
  691.6 7.1 copy-start
  738.3 6.4 copy-start
  752.0 134.3 %reduce-scatter.20.cloned.1.call-start = ((), (), s32[]{:S(2)}) async-start(), calls=%async_computation.20 | async-start | bytes 2654208 | tf_op jit(solution)/shard_map/reduce_scatter | solution.py:276
  752.1 4.7 copy-start.48
  760.9 262.9 %reduce-scatter.26.cloned.1.call-start = ((), (), s32[]{:S(2)}) async-start(), calls=%async_computation.23 | async-start | bytes 2162688 | tf_op jit(solution)/shard_map/reduce_scatter | solution.py:281
  765.8 294.6 %reduce-scatter.18.cloned.1.call-start = ((), (), s32[]{:S(2)}) async-start(), calls=%async_computation.19 | async-start | bytes 3932160 | tf_op jit(solution)/shard_map/reduce_scatter | solution.py:265
  772.6 43.1 %copy-start.26 = (f32[192,96]{1,0:T(8,128)S(1)}, f32[192,96]{1,0:T(8,128)}, u32[]{:S(2)}) copy-start(f32[192,96]{1,0:T(8,128)} %param.33) | copy-start | bytes 221188
  772.6 43.1 %copy-start.35 = (f32[192,96]{1,0:T(8,128)S(1)}, f32[192,96]{1,0:T(8,128)}, u32[]{:S(2)}) copy-start(f32[192,96]{1,0:T(8,128)} %param.45) | copy-start | bytes 221188
  772.6 43.1 %copy-start.36 = (f32[192,96]{1,0:T(8,128)S(1)}, f32[192,96]{1,0:T(8,128)}, u32[]{:S(2)}) copy-start(f32[192,96]{1,0:T(8,128)} %param.39) | copy-start | bytes 221188
  773.2 113.1 %copy-start.19 = (f32[96,3,192]{2,0,1:T(8,128)S(1)}, f32[96,3,192]{2,0,1:T(8,128)}, u32[]{:S(2)}) copy-start(f32[96,3,192]{2,0,1:T(8,128)} %param.32) | copy-start | bytes 663556
  773.2 113.1 %copy-start.32 = (f32[96,3,192]{2,0,1:T(8,128)S(1)}, f32[96,3,192]{2,0,1:T(8,128)}, u32[]{:S(2)}) copy-start(f32[96,3,192]{2,0,1:T(8,128)} %param.44) | copy-start | bytes 663556
  773.2 113.1 %copy-start.33 = (f32[96,3,192]{2,0,1:T(8,128)S(1)}, f32[96,3,192]{2,0,1:T(8,128)}, u32[]{:S(2)}) copy-start(f32[96,3,192]{2,0,1:T(8,128)} %param.38) | copy-start | bytes 663556
  815.7 208.1 %copy-start.34 = (f32[64,256]{1,0:T(8,128)S(1)}, f32[64,256]{1,0:T(8,128)}, u32[]{:S(2)}) copy-start(f32[64,256]{1,0:T(8,128)} %param.36) | copy-start | bytes 196612
  815.7 208.1 %copy-start.39 = (f32[64,256]{1,0:T(8,128)S(1)}, f32[64,256]{1,0:T(8,128)}, u32[]{:S(2)}) copy-start(f32[64,256]{1,0:T(8,128)} %param.48) | copy-start | bytes 196612
  815.7 208.1 %copy-start.40 = (f32[64,256]{1,0:T(8,128)S(1)}, f32[64,256]{1,0:T(8,128)}, u32[]{:S(2)}) copy-start(f32[64,256]{1,0:T(8,128)} %param.42) | copy-start | bytes 196612
  816.5 243.8 %copy-start.3 = (bf16[1,512,768]{2,1,0:T(8,128)(2,1)S(1)}, bf16[1,512,768]{2,1,0:T(8,128)(2,1)}, u32[]{:S(2)}) copy-start(bf16[1,512,768]{2,1,0:T(8,128)(2,1)} %param.29) | copy-start | bytes 2359300
  816.5 243.8 %copy-start.38 = (f32[768]{0:T(1024)S(1)}, f32[768]{0:T(1024)}, u32[]{:S(2)}) copy-start(f32[768]{0:T(1024)} %copy-done.37) | copy-start | bytes 9220
  816.5 243.8 %copy-start.42 = (f32[512]{0:T(512)S(1)}, f32[512]{0:T(512)}, u32[]{:S(2)}) copy-start(f32[512]{0:T(512)} %copy-done.41) | copy-start | bytes 6148
  888.5 218.3 %copy-start.43 = (f32[2,768]{1,0:T(2,128)S(1)}, f32[2,768]{1,0:T(2,128)}, u32[]{:S(2)}) copy-start(f32[2,768]{1,0:T(2,128)} %param.37) | copy-start | bytes 18436
  888.5 218.3 %copy-start.46 = (f32[2,768]{1,0:T(2,128)S(1)}, f32[2,768]{1,0:T(2,128)}, u32[]{:S(2)}) copy-start(f32[2,768]{1,0:T(2,128)} %param.49) | copy-start | bytes 18436
  888.5 218.3 %copy-start.47 = (f32[2,768]{1,0:T(2,128)S(1)}, f32[2,768]{1,0:T(2,128)}, u32[]{:S(2)}) copy-start(f32[2,768]{1,0:T(2,128)} %param.43) | copy-start | bytes 18436
  888.5 219.0 %copy-start.7 = (f32[1,512,768]{2,1,0:T(8,128)S(1)}, f32[1,512,768]{2,1,0:T(8,128)}, u32[]{:S(2)}) copy-start(f32[1,512,768]{2,1,0:T(8,128)} %get-tuple-element.374) | copy-start | bytes 4718596
  (30 other events, 58.6 us)
Sparse Core Ops, SparseCore 0:
  11.7 63.4 all-gather.9
  77.4 27.9 all-gather.7
  168.2 58.4 reduce-scatter.11
  526.0 28.5 all-gather.19
Sparse Core Ops, SparseCore 1:
  171.3 41.5 all-gather.13
  229.5 28.3 all-gather.11
  259.4 28.3 all-gather.17
  296.2 69.0 reduce-scatter.23
  368.2 40.6 all-gather.15
  423.6 56.7 reduce-scatter.15
  482.7 37.8 reduce-scatter.13
  538.3 69.0 reduce-scatter.21
  752.1 62.5 reduce-scatter.27
  818.2 68.1 reduce-scatter.19
  888.5 135.3 reduce-scatter.25
  1026.6 33.7 reduce-scatter.17
where the time goes:
time: 1130 us; the launch traced here: 1120 us
  waiting for transfers between devices  613 us (54%)
  local copies, waits for them, and re-layouts  194 us (17%)
  matrix products  119 us (11%)
  blocking collectives  111 us (10%)
  other arithmetic  54.9 us (5%)
  between operations  17.4 us (2%)
    reduce_scatter x1, waiting for transfers between devices, shards(): lax.psum_scatter(grad_bias_local, ('dp', 'mp'), scatter_dimension=0, tile...  135 us
    reduce_scatter x1, waiting for transfers between devices, shards(): lax.psum_scatter(grad_projection, 'dp', scatter_dimension=0, tiled=True)  69.8 us
    reduce_scatter x1, waiting for transfers between devices, shards(): lax.psum_scatter(grad_down_local, 'dp', scatter_dimension=1, tiled=True)  69.1 us
    concatenate x4, local copies, waits for them, and re-layouts, unskew_band(): jnp.concatenate([band_grad.reshape(-1), jnp.zeros((height,), band_grad.dt...  65 us
    reduce_scatter x1, waiting for transfers between devices, shards(): lax.psum_scatter(attn_terms, 'mp', scatter_dimension=1, tiled=True)  56.4 us
    reduce_scatter x1, waiting for transfers between devices, shards(): lax.psum_scatter(normed_terms, 'mp', scatter_dimension=1, tiled=True)  47 us
    all_gather x1, waiting for transfers between devices, shards(): lax.all_gather(w_down.astype(jnp.bfloat16), 'dp', axis=1, tiled=True)  41.4 us
    all_gather x1, blocking collectives, shards(): lax.all_gather(w_qkv.astype(jnp.bfloat16), 'dp', axis=0, tiled=True)  40.4 us
  transfers between devices with their start and end apart: 16, of which 13 were waited for; matrix products, arithmetic and copies ran while one was open for 23% of the time, Pallas kernels for 0%

commit v1 on v0

--- a/solution.py
+++ b/solution.py
@@ -11,6 +11,31 @@
 LEARN_RATE = 0.03
 WEIGHT_DECAY = 0.1
 ADAM_EPS = 1e-08
+
+
+def fix_thing(shard_in):
+    passed = jax.lax.axis_size("dp")
+    taken_in = jax.lax.axis_index("dp")
+    piece_now, mat_out, after = (passed, taken_in, shard_in.shape[0])
+    sheets = tuple((c * piece_now if to_i == 0 else c for to_i, c in enumerate(shard_in.shape)))
+    k_now = lax.dynamic_update_slice_in_dim(
+        jnp.zeros(sheets, shard_in.dtype), shard_in, mat_out * after, axis=0
+    )
+    o_now = top = shard_in
+    for idx in range(1, piece_now // 2 + 1):
+        o_now = jax.lax.ppermute(
+            o_now, "dp", perm=tuple(((to_i, (to_i + 1) % piece_now) for to_i in range(piece_now)))
+        )
+        k_now = lax.dynamic_update_slice_in_dim(
+            k_now, o_now, (mat_out - idx) % piece_now * after, axis=0
+        )
+        if 2 * idx < piece_now:
+            kept_arr = tuple(((to_i, (to_i - 1) % piece_now) for to_i in range(piece_now)))
+            top = jax.lax.ppermute(top, "dp", kept_arr)
+            k_now = lax.dynamic_update_slice_in_dim(
+                k_now, top, (mat_out + idx) % piece_now * after, axis=0
+            )
+    return k_now
 
 
 def skew_band(bias_rows):
@@ -175,7 +200,7 @@
     second_gains,
 ):
     query_weights, mixer_weights, hidden_weights, back_weights = (
-        lax.all_gather(w_qkv.astype(jnp.bfloat16), "dp", axis=0, tiled=True),
+        fix_thing(w_qkv.astype(jnp.bfloat16)),
         lax.all_gather(w_out.astype(jnp.bfloat16), "dp", axis=1, tiled=True),
         lax.all_gather(w_up.astype(jnp.bfloat16), "dp", axis=0, tiled=True),
         lax.all_gather(w_down.astype(jnp.bfloat16), "dp", axis=1, tiled=True),

time: 1130 us -> 1120 us (level)
  blocking collectives: 111 us -> 75.4 us
  starting transfers between devices: 1.33 us -> 18.5 us
    all_gather x1 -> x0, blocking collectives: 40.4 us -> none  [shards(): lax.all_gather(w_qkv.astype(jnp.bfloat16), 'dp', axis=0, tiled=True)]
    ppermute x0 -> x7, starting transfers between devices: none -> 17.3 us  [the longest x3 12.5 us: fix_thing(): top = jax.lax.ppermute(top, 'dp', kept_arr)]
  transfers between devices with their start and end apart: 16 -> 23, of which waited for: 13 -> 16; matrix products, arithmetic and copies ran while one was open for 23% -> 24% of each run, Pallas kernels for 0% -> 0%
where the time goes in v1:
time: 1120 us
  waiting for transfers between devices  620 us (55%)
  local copies, waits for them, and re-layouts  203 us (18%)
  matrix products  119 us (11%)
  blocking collectives  75.4 us (7%)
  other arithmetic  55.1 us (5%)
  starting transfers between devices  18.5 us (2%)
  between operations  17.7 us (2%)
    reduce_scatter x1, waiting for transfers between devices, shards(): lax.psum_scatter(grad_bias_local, ('dp', 'mp'), scatter_dimension=0, tile...  136 us
    reduce_scatter x1, waiting for transfers between devices, shards(): lax.psum_scatter(grad_projection, 'dp', scatter_dimension=0, tiled=True)  69.6 us
    reduce_scatter x1, waiting for transfers between devices, shards(): lax.psum_scatter(grad_down_local, 'dp', scatter_dimension=1, tiled=True)  69.1 us
    concatenate x4, local copies, waits for them, and re-layouts, unskew_band(): jnp.concatenate([band_grad.reshape(-1), jnp.zeros((height,), band_grad.dt...  65 us
    reduce_scatter x1, waiting for transfers between devices, shards(): lax.psum_scatter(attn_terms, 'mp', scatter_dimension=1, tiled=True)  56.9 us
    reduce_scatter x1, waiting for transfers between devices, shards(): lax.psum_scatter(normed_terms, 'mp', scatter_dimension=1, tiled=True)  47 us
    all_gather x1, waiting for transfers between devices, shards(): lax.all_gather(w_down.astype(jnp.bfloat16), 'dp', axis=1, tiled=True)  41.4 us
    unnamed x17, waiting for transfers between devices  39.8 us
  transfers between devices with their start and end apart: 23, of which 16 were waited for; matrix products, arithmetic and copies ran while one was open for 24% of the time, Pallas kernels for 0%

profile of v1, /device:TPU:0, one launch (start us, length us, event | category | flops | bytes accessed | tf_op | source)
XLA Modules:
  0.0 1115.8 jit_solution(594434238190717274)
XLA Ops:
  19.6 3.9 collective-permute-done
  25.3 4.0 collective-permute-start.3
  33.0 5.4 collective-permute-start.5
  39.8 36.0 %all_gather.26 = bf16[192,768]{0,1:T(8,128)(2,1)S(1)} all-gather(bf16[192,96]{0,1:T(8,128)(2,1)S(1)} %copy.97), channel_id=1, replica_groups=mesh['dp'=8,'mp'=4] {'dp'}, dimensions={1}, use_global_device_ids=true | all-gather | bytes 331776 | tf_op jit(solution)/shard_map/all_gather | solution.py:204
  85.3 3.1 exponential_convert_fusion
  88.4 14.6 %all-gather.8.cloned.1.call-done = bf16[1,2048,768]{2,1,0:T(8,128)(2,1)} async-done(((bf16[1,512,768]{2,1,0:T(8,128)(2,1)}), bf16[1,2048,768]{2,1,0:T(8,128)(2,1)}) %all-gather.8.cloned.1.call-update) | async-done | bytes 3145744 | tf_op jit(solution)/shard_map/all_gather | solution.py:218
  103.0 3.9 fusion.52
  113.2 40.6 %while.36 = (s32[]{:T(128)}, f32[4,1,512,192]{2,3,1,0:T(8,128)}, f32[4,1,512,192]{2,3,1,0:T(8,128)}, s32[4]{0:T(128)S(1)}, bf16[2048,256]{1,0:T(8,128)(2,1)}, /*...) while((s32[]{:T(128)}, f32[4,1,512,192]{2,3,1,0:T(8,128)}, ...), condition=%wide.region_2.3_spmd, body=%wide.region_1.2_spmd.sunk | while | flops 304352256 | bytes 9974028 | solution.py:78
  160.5 5.7 convolution_bitcast_fusion.2
  167.8 56.9 %reduce-scatter.12.cloned.1.call-done = f32[1,512,768]{2,1,0:T(8,128)} async-done(((f32[1,2048,768]{2,1,0:T(8,128)}), f32[1,512,768]{2,1,0:T(8,128)}) %reduce-scatter.12.cloned.1.call-update) | async-done | bytes 1572880 | tf_op jit(solution)/shard_map/reduce_scatter | solution.py:232
  229.6 26.4 %all-gather.12.cloned.1.call-done = bf16[1,2048,768]{2,1,0:T(8,128)(2,1)} async-done(((bf16[1,512,768]{2,1,0:T(8,128)(2,1)}), bf16[1,2048,768]{2,1,0:T(8,128)(2,1)}) %all-gather.12.cloned.1.call-update) | async-done | bytes 3145744 | tf_op jit(solution)/shard_map/all_gather | solution.py:236
  256.0 7.5 fusion.50
  263.5 22.4 %all-gather.18.cloned.1.call-done = bf16[1,2048,768]{2,1,0:T(8,128)(2,1)} async-done(((bf16[1,512,768]{2,1,0:T(8,128)(2,1)}), bf16[1,2048,768]{2,1,0:T(8,128)(2,1)}) %all-gather.18.cloned.1.call-update) | async-done | bytes 3145744 | tf_op jit(solution)/shard_map/all_gather | solution.py:248
  285.9 8.3 fusion.44
  294.3 69.1 %reduce-scatter.24.cloned.1.call-done = f32[768,96]{0,1:T(8,128)} async-done(((f32[768,768]{0,1:T(8,128)}), f32[768,96]{0,1:T(8,128)}) %reduce-scatter.24.cloned.1.call-update) | async-done | bytes 294928 | tf_op jit(solution)/shard_map/reduce_scatter | solution.py:304
  365.6 41.4 %all-gather.16.cloned.1.call-done = bf16[768,768]{0,1:T(8,128)(2,1)} async-done(((bf16[768,96]{0,1:T(8,128)(2,1)}), bf16[768,768]{0,1:T(8,128)(2,1)}) %all-gather.16.cloned.1.call-update) | async-done | bytes 1179664 | tf_op jit(solution)/shard_map/all_gather | solution.py:206
  407.0 8.2 fusion.37
  417.1 4.6 convolution_bitcast_fusion.3
  422.9 8.5 fusion.54
  431.5 47.0 %reduce-scatter.16.cloned.1.call-done = f32[1,512,768]{2,1,0:T(8,128)} async-done(((f32[1,2048,768]{2,1,0:T(8,128)}), f32[1,512,768]{2,1,0:T(8,128)}) %reduce-scatter.16.cloned.1.call-update) | async-done | bytes 1572880 | tf_op jit(solution)/shard_map/reduce_scatter | solution.py:256
  480.9 37.8 %reduce-scatter.14.cloned.1.call-done = bf16[1,512,768]{2,1,0:T(8,128)(2,1)} async-done(((bf16[1,2048,768]{2,1,0:T(8,128)(2,1)}), bf16[1,512,768]{2,1,0:T(8,128)(2,1)}) %reduce-scatter.14.cloned.1.call-update) | async-done | bytes 786448 | tf_op jit(solution)/shard_map/reduce_scatter | solution.py:242
  518.7 5.3 fusion.105
  524.1 3.3 div.149
  532.1 4.2 fusion.48
  536.4 16.4 %all-gather.20.cloned.1.call-done = bf16[1,2048,768]{2,1,0:T(8,128)(2,1)} async-done(((bf16[1,512,768]{2,1,0:T(8,128)(2,1)}), bf16[1,2048,768]{2,1,0:T(8,128)(2,1)}) %all-gather.20.cloned.1.call-update) | async-done | bytes 3145744 | tf_op jit(solution)/shard_map/all_gather | solution.py:265
  552.8 5.9 fusion.96
  563.7 186.3 %while.37 = (s32[]{:T(128)}, f32[1,2304,192]{1,2,0:T(8,128)}, f32[1,2304,192]{1,2,0:T(8,128)}, f32[4,1,512,256]{3,2,1,0:T(8,128)}, s32[4]{0:T(128)S(1)}, /*index...) while((s32[]{:T(128)}, f32[1,2304,192]{1,2,0:T(8,128)}, ...), condition=%wide.region_10.11_spmd, body=%wide.region_8.10_spmd.sunk | while | flops 607325184 | bytes 47336400 | solution.py:142
  570.2 16.3 %pad_reduce_fusion.2 = f32[393728]{0:T(1024)S(1)} fusion(f32[1,393216]{1,0:T(1,128)S(1)} %bitcast.305), kind=kLoop, calls=%fused_computation.13.clone.1 | loop fusion | bytes 3147776 | tf_op jit(solution)/shard_map/vmap()/while/body/eval_jaxpr/concatenate | solution.py:56
  597.6 4.4 scatter.13
  604.1 5.9 scatter.12
  617.5 16.3 %pad_reduce_fusion.2 = f32[393728]{0:T(1024)S(1)} fusion(f32[1,393216]{1,0:T(1,128)S(1)} %bitcast.305), kind=kLoop, calls=%fused_computation.13.clone.1 | loop fusion | bytes 3147776 | tf_op jit(solution)/shard_map/vmap()/while/body/eval_jaxpr/concatenate | solution.py:56
  644.9 4.4 scatter.13
  651.4 5.9 scatter.12
  664.9 16.3 %pad_reduce_fusion.2 = f32[393728]{0:T(1024)S(1)} fusion(f32[1,393216]{1,0:T(1,128)S(1)} %bitcast.305), kind=kLoop, calls=%fused_computation.13.clone.1 | loop fusion | bytes 3147776 | tf_op jit(solution)/shard_map/vmap()/while/body/eval_jaxpr/concatenate | solution.py:56
  692.3 4.3 scatter.13
  698.7 5.3 scatter.12
  711.5 16.3 %pad_reduce_fusion.2 = f32[393728]{0:T(1024)S(1)} fusion(f32[1,393216]{1,0:T(1,128)S(1)} %bitcast.305), kind=kLoop, calls=%fused_computation.13.clone.1 | loop fusion | bytes 3147776 | tf_op jit(solution)/shard_map/vmap()/while/body/eval_jaxpr/concatenate | solution.py:56
  738.9 3.7 scatter.13
  744.7 3.9 scatter.12
  750.1 3.7 fusion.94
  754.8 4.1 fusion.38
  760.5 3.3 bitcast_multiply_fusion
  765.2 5.4 fusion.55
  773.9 38.9 %reduce-scatter.28.cloned.1.call-done = f32[96,192]{1,0:T(8,128)} async-done(((f32[768,192]{1,0:T(8,128)}), f32[96,192]{1,0:T(8,128)}) %reduce-scatter.28.cloned.1.call-update) | async-done | bytes 73744
  814.6 69.6 %reduce-scatter.20.cloned.1.call-done = f32[96,3,192]{2,0,1:T(8,128)} async-done(((f32[768,3,192]{2,0,1:T(8,128)}), f32[96,3,192]{2,0,1:T(8,128)}) %reduce-scatter.20.cloned.1.call-update) | async-done | bytes 221200 | tf_op jit(solution)/shard_map/reduce_scatter | solution.py:301
  886.4 135.7 %reduce-scatter.26.cloned.1.call-done = f32[64,256]{1,0:T(8,128)} async-done(((f32[2048,256]{1,0:T(8,128)}), f32[64,256]{1,0:T(8,128)}) %reduce-scatter.26.cloned.1.call-update) | async-done | bytes 65552 | tf_op jit(solution)/shard_map/reduce_scatter | solution.py:306
  1023.6 34.9 %reduce-scatter.18.cloned.1.call-done = bf16[1,512,768]{2,1,0:T(8,128)(2,1)} async-done(((bf16[1,2048,768]{2,1,0:T(8,128)(2,1)}), bf16[1,512,768]{2,1,0:T(8,128)(2,1)}) %reduce-scatter.18.cloned.1.call-update) | async-done | bytes 786448 | tf_op jit(solution)/shard_map/reduce_scatter | solution.py:290
  1063.8 39.4 %all-reduce.3 = (f32[2,768]{1,0:T(2,128)S(1)}, f32[4]{0:T(128)S(1)}) all-reduce(f32[2,768]{1,0:T(2,128)S(1)} %pad_maximum_fusion.3, f32[4]{0:T(128)S(1)} %pad_maximum_fusion.4), channel_id=1, replica_groups=mesh['dp'=8,'mp'=4] {'dp','mp'}, use_global_device_ids=true, to_apply=%region_20.21 | all-reduce | flops 1540 | bytes 12320 | tf_op jit(solution)/shard_map/psum | solution.py:316
  (379 shorter events, 203.7 us)
Async XLA Ops:
  8.0 77.3 %all-gather.10.cloned.1.call-start = ((), (), s32[]{:S(2)}) async-start(), calls=%async_computation.10 | async-start | bytes 2162688 | tf_op jit(solution)/shard_map/all_gather | solution.py:208
  8.8 94.2 %all-gather.8.cloned.1.call-start = ((), (), s32[]{:S(2)}) async-start(), calls=%async_computation.9 | async-start | bytes 3932160 | tf_op jit(solution)/shard_map/all_gather | solution.py:218
  11.1 21.1 %copy-start.25 = (f32[192,96]{1,0:T(8,128)S(1)}, f32[192,96]{1,0:T(8,128)}, u32[]{:S(2)}) copy-start(f32[192,96]{1,0:T(8,128)} %param.33) | copy-start | bytes 221188
  13.4 211.3 %reduce-scatter.12.cloned.1.call-start = ((), (), s32[]{:S(2)}) async-start(), calls=%async_computation.11 | async-start | bytes 7864320 | tf_op jit(solution)/shard_map/reduce_scatter | solution.py:232
  13.5 10.0 collective-permute-start
  16.5 8.7 collective-permute-start.1
  23.5 8.3 collective-permute-start.2
  25.3 7.7 collective-permute-start.3
  31.8 7.9 collective-permute-start.4
  33.0 50.0 %collective-permute-start.5 = (bf16[96,3,192]{2,0,1:T(8,128)(2,1)S(1)}, bf16[96,3,192]{2,0,1:T(8,128)(2,1)S(1)}, u32[]{:S(2)}, u32[]{:S(2)}) collective-permute-start(bf16[96,3,192]{2,0,1:T(8,128)(2,1)S(1)} %collective-permute-done.3), channel_id=1, source_target_pairs={{0,28},{4,0},{8,4},{12,8},{16,12},{20,16},{24,20},{28,24},{1,29},{... | collective-permute-start | bytes 331784 | tf_op jit(solution)/shard_map/ppermute | solution.py:34
  39.8 44.7 %collective-permute-start.6 = (bf16[96,3,192]{2,0,1:T(8,128)(2,1)S(1)}, bf16[96,3,192]{2,0,1:T(8,128)(2,1)S(1)}, u32[]{:S(2)}, u32[]{:S(2)}) collective-permute-start(bf16[96,3,192]{2,0,1:T(8,128)(2,1)S(1)} %collective-permute-done.4), channel_id=1, source_target_pairs={{0,4},{4,8},{8,12},{12,16},{16,20},{20,24},{24,28},{28,0},{1,5},{5... | collective-permute-start | bytes 331784 | tf_op jit(solution)/shard_map/ppermute | solution.py:26
  85.3 17.7 %copy-start.20 = (bf16[768,3,192]{0,2,1:T(8,128)(2,1)}, bf16[768,3,192]{0,2,1:T(8,128)(2,1)S(1)}, u32[]{:S(2)}) copy-start(bf16[768,3,192]{0,2,1:T(8,128)(2,1)S(1)} %dynamic_update_slice.42) | copy-start | bytes 2654212
  166.1 58.6 %copy-start.2 = (bf16[1,512,768]{2,1,0:T(8,128)(2,1)S(1)}, bf16[1,512,768]{2,1,0:T(8,128)(2,1)}, u32[]{:S(2)}) copy-start(bf16[1,512,768]{2,1,0:T(8,128)(2,1)} %param.29) | copy-start | bytes 2359300
  166.1 63.5 %all-gather.14.cloned.1.call-start = ((), (), s32[]{:S(2)}) async-start(), calls=%async_computation.13 | async-start | bytes 1327104 | tf_op jit(solution)/shard_map/all_gather | solution.py:205
  167.8 88.2 %all-gather.12.cloned.1.call-start = ((), (), s32[]{:S(2)}) async-start(), calls=%async_computation.12 | async-start | bytes 3932160 | tf_op jit(solution)/shard_map/all_gather | solution.py:236
  227.5 58.4 %all-gather.18.cloned.1.call-start = ((), (), s32[]{:S(2)}) async-start(), calls=%async_computation.16 | async-start | bytes 3932160 | tf_op jit(solution)/shard_map/all_gather | solution.py:248
  229.4 134.0 %reduce-scatter.24.cloned.1.call-start = ((), (), s32[]{:S(2)}) async-start(), calls=%async_computation.22 | async-start | bytes 2654208 | tf_op jit(solution)/shard_map/reduce_scatter | solution.py:304
  294.2 69.2 %copy-start.27 = (f32[768,96]{0,1:T(8,128)S(1)}, f32[768,96]{0,1:T(8,128)}, u32[]{:S(2)}) copy-start(f32[768,96]{0,1:T(8,128)} %param.35) | copy-start | bytes 884740
  294.2 69.2 %copy-start.28 = (f32[768,96]{0,1:T(8,128)S(1)}, f32[768,96]{0,1:T(8,128)}, u32[]{:S(2)}) copy-start(f32[768,96]{0,1:T(8,128)} %param.47) | copy-start | bytes 884740
  294.2 69.2 %copy-start.29 = (f32[768,96]{0,1:T(8,128)S(1)}, f32[768,96]{0,1:T(8,128)}, u32[]{:S(2)}) copy-start(f32[768,96]{0,1:T(8,128)} %param.41) | copy-start | bytes 884740
  294.2 112.8 %all-gather.16.cloned.1.call-start = ((), (), s32[]{:S(2)}) async-start(), calls=%async_computation.14 | async-start | bytes 1327104 | tf_op jit(solution)/shard_map/all_gather | solution.py:206
  365.6 51.5 %copy-start.51 = (bf16[768,768]{1,0:T(8,128)(2,1)S(1)}, bf16[768,768]{1,0:T(8,128)(2,1)}, u32[]{:S(2)}) copy-start(bf16[768,768]{1,0:T(8,128)(2,1)} %all-gather.14.cloned.1.call-done) | copy-start | bytes 3538948
  365.6 112.9 %reduce-scatter.16.cloned.1.call-start = ((), (), s32[]{:S(2)}) async-start(), calls=%async_computation.17 | async-start | bytes 7864320 | tf_op jit(solution)/shard_map/reduce_scatter | solution.py:256
  421.7 97.1 %reduce-scatter.14.cloned.1.call-start = ((), (), s32[]{:S(2)}) async-start(), calls=%async_computation.15 | async-start | bytes 3932160 | tf_op jit(solution)/shard_map/reduce_scatter | solution.py:242
  431.5 87.3 %copy-start.6 = (f32[1,512,768]{2,1,0:T(8,128)S(1)}, f32[1,512,768]{2,1,0:T(8,128)}, u32[]{:S(2)}) copy-start(f32[1,512,768]{2,1,0:T(8,128)} %reduce-scatter.12.cloned.1.call-done) | copy-start | bytes 4718596
  431.5 121.3 %all-gather.20.cloned.1.call-start = ((), (), s32[]{:S(2)}) async-start(), calls=%async_computation.18 | async-start | bytes 3932160 | tf_op jit(solution)/shard_map/all_gather | solution.py:265
  524.1 247.2 %reduce-scatter.22.cloned.1.call-start = ((), (), s32[]{:S(2)}) async-start(), calls=%async_computation.21 | async-start | bytes 2654208 | tf_op jit(solution)/shard_map/reduce_scatter | solution.py:303
  532.1 20.6 %copy-start.15 = (f32[24,8,4,512]{3,1,2,0:T(8,128)S(1)}, f32[24,8,4,512]{3,1,2,0:T(8,128)}, u32[]{:S(2)}) copy-start(f32[24,8,4,512]{3,1,2,0:T(8,128)} %copy-done.14) | copy-start | bytes 4718596
  536.3 276.4 %reduce-scatter.28.cloned.1.call-start = ((), (), s32[]{:S(2)}) async-start(), calls=%async_computation.24 | async-start | bytes 884736
  750.0 134.2 %reduce-scatter.20.cloned.1.call-start = ((), (), s32[]{:S(2)}) async-start(), calls=%async_computation.20 | async-start | bytes 2654208 | tf_op jit(solution)/shard_map/reduce_scatter | solution.py:301
  758.9 263.2 %reduce-scatter.26.cloned.1.call-start = ((), (), s32[]{:S(2)}) async-start(), calls=%async_computation.23 | async-start | bytes 2162688 | tf_op jit(solution)/shard_map/reduce_scatter | solution.py:306
  763.8 294.8 %reduce-scatter.18.cloned.1.call-start = ((), (), s32[]{:S(2)}) async-start(), calls=%async_computation.19 | async-start | bytes 3932160 | tf_op jit(solution)/shard_map/reduce_scatter | solution.py:290
  770.6 43.1 %copy-start.26 = (f32[192,96]{1,0:T(8,128)S(1)}, f32[192,96]{1,0:T(8,128)}, u32[]{:S(2)}) copy-start(f32[192,96]{1,0:T(8,128)} %param.33) | copy-start | bytes 221188
  770.6 43.1 %copy-start.35 = (f32[192,96]{1,0:T(8,128)S(1)}, f32[192,96]{1,0:T(8,128)}, u32[]{:S(2)}) copy-start(f32[192,96]{1,0:T(8,128)} %param.45) | copy-start | bytes 221188
  770.6 43.1 %copy-start.36 = (f32[192,96]{1,0:T(8,128)S(1)}, f32[192,96]{1,0:T(8,128)}, u32[]{:S(2)}) copy-start(f32[192,96]{1,0:T(8,128)} %param.39) | copy-start | bytes 221188
  771.3 113.0 %copy-start.19 = (f32[96,3,192]{2,0,1:T(8,128)S(1)}, f32[96,3,192]{2,0,1:T(8,128)}, u32[]{:S(2)}) copy-start(f32[96,3,192]{2,0,1:T(8,128)} %param.32) | copy-start | bytes 663556
  771.3 113.0 %copy-start.32 = (f32[96,3,192]{2,0,1:T(8,128)S(1)}, f32[96,3,192]{2,0,1:T(8,128)}, u32[]{:S(2)}) copy-start(f32[96,3,192]{2,0,1:T(8,128)} %param.44) | copy-start | bytes 663556
  771.3 113.0 %copy-start.33 = (f32[96,3,192]{2,0,1:T(8,128)S(1)}, f32[96,3,192]{2,0,1:T(8,128)}, u32[]{:S(2)}) copy-start(f32[96,3,192]{2,0,1:T(8,128)} %param.38) | copy-start | bytes 663556
  813.8 208.3 %copy-start.34 = (f32[64,256]{1,0:T(8,128)S(1)}, f32[64,256]{1,0:T(8,128)}, u32[]{:S(2)}) copy-start(f32[64,256]{1,0:T(8,128)} %param.36) | copy-start | bytes 196612
  813.8 208.3 %copy-start.39 = (f32[64,256]{1,0:T(8,128)S(1)}, f32[64,256]{1,0:T(8,128)}, u32[]{:S(2)}) copy-start(f32[64,256]{1,0:T(8,128)} %param.48) | copy-start | bytes 196612
  813.8 208.3 %copy-start.40 = (f32[64,256]{1,0:T(8,128)S(1)}, f32[64,256]{1,0:T(8,128)}, u32[]{:S(2)}) copy-start(f32[64,256]{1,0:T(8,128)} %param.42) | copy-start | bytes 196612
  814.6 244.0 %copy-start.3 = (bf16[1,512,768]{2,1,0:T(8,128)(2,1)S(1)}, bf16[1,512,768]{2,1,0:T(8,128)(2,1)}, u32[]{:S(2)}) copy-start(bf16[1,512,768]{2,1,0:T(8,128)(2,1)} %param.29) | copy-start | bytes 2359300
  814.6 244.0 %copy-start.38 = (f32[768]{0:T(1024)S(1)}, f32[768]{0:T(1024)}, u32[]{:S(2)}) copy-start(f32[768]{0:T(1024)} %copy-done.37) | copy-start | bytes 9220
  814.6 244.0 %copy-start.42 = (f32[512]{0:T(512)S(1)}, f32[512]{0:T(512)}, u32[]{:S(2)}) copy-start(f32[512]{0:T(512)} %copy-done.41) | copy-start | bytes 6148
  886.4 218.6 %copy-start.43 = (f32[2,768]{1,0:T(2,128)S(1)}, f32[2,768]{1,0:T(2,128)}, u32[]{:S(2)}) copy-start(f32[2,768]{1,0:T(2,128)} %param.37) | copy-start | bytes 18436
  886.4 218.6 %copy-start.46 = (f32[2,768]{1,0:T(2,128)S(1)}, f32[2,768]{1,0:T(2,128)}, u32[]{:S(2)}) copy-start(f32[2,768]{1,0:T(2,128)} %param.49) | copy-start | bytes 18436
  886.4 218.6 %copy-start.47 = (f32[2,768]{1,0:T(2,128)S(1)}, f32[2,768]{1,0:T(2,128)}, u32[]{:S(2)}) copy-start(f32[2,768]{1,0:T(2,128)} %param.43) | copy-start | bytes 18436
  886.4 219.2 %copy-start.7 = (f32[1,512,768]{2,1,0:T(8,128)S(1)}, f32[1,512,768]{2,1,0:T(8,128)}, u32[]{:S(2)}) copy-start(f32[1,512,768]{2,1,0:T(8,128)} %get-tuple-element.357) | copy-start | bytes 4718596
  (37 other events, 120.7 us)
Sparse Core Ops, SparseCore 0:
  11.7 61.8 all-gather.9
  75.7 27.2 all-gather.7
  166.3 58.4 reduce-scatter.11
  524.2 28.5 all-gather.19
Sparse Core Ops, SparseCore 1:
  169.4 41.5 all-gather.13
  227.6 28.3 all-gather.11
  257.5 28.3 all-gather.17
  294.3 69.0 reduce-scatter.23
  366.4 40.6 all-gather.15
  421.8 56.7 reduce-scatter.15
  480.9 37.8 reduce-scatter.13
  536.4 69.0 reduce-scatter.21
  750.1 62.6 reduce-scatter.27
  816.3 67.9 reduce-scatter.19
  886.4 135.7 reduce-scatter.25
  1024.8 33.7 reduce-scatter.17
